TPU v7x, 32 devices: a whole 2x2x4 slice. The times are simulated.
32 devices in a mesh: coarse: 4 (over z), member: 8 (over y, x, core).
Axes of the slice: x: 2, y: 2, z: 4, core: 2. Of those that a mesh axis runs over, the one named last changes fastest.
Arguments:
- samples: bfloat16 [40960, 768], P(('coarse', 'member')), may hold values from -6 to 6
- coarse_label: int32 [40960, 1], P(('coarse', 'member')), may hold values from 0 to 3; in each aligned block of 1280 rows (0 to 1279, 1280 to 2559, ...) at most 480 rows name the same one
- fine_label: int32 [40960], P(('coarse', 'member')), may hold values from 0 to 1023
- live_rows: int32 [32], P(('coarse', 'member')), may hold values from 1 to 1280, 30720 in all
- old_centroids: float32 [4, 1024, 768], P('coarse'), may hold values from -0.3 to 0.3
Outputs:
- scores: bfloat16 [40960, 1024], P(('coarse', 'member'))
- new_centroids: float32 [4, 1024, 768], P('coarse', 'member')
Inputs may be any that keep to these rules, and one draw needn't show every extreme that they name: `coarse_label`: among the rows of one device no group is named more than 480 times; some group reaches 480 on some devices. `live_rows`: the largest value equals 1280.
All inputs are finite; a program needn't handle non-finite values. No bound on the sum of `live_rows` on one device may be relied on, other than what follows from the above.
Results may differ from a plain program's by a relative error of at most 0.0085.
Values may be sent and summed in bfloat16 or wider, within the bound.
No kernel may reach another device: no remote copies, remote signals or barrier semaphores. Data moves between devices by JAX's collectives and lax.ppermute only.
A program may use at most 64 MiB of HBM per device.

v0:
```python
import jax
import jax.numpy as jnp
from jax import lax
from jax.sharding import PartitionSpec as P

CAP = 480
prior_weight = 16.0


def per_device(samples, coarse_label, fine_label, live_rows, old_centroids):
    groups = lax.axis_size("coarse")
    members = lax.axis_size("member")
    member_index = lax.axis_index("member")
    row_count = samples.shape[0]
    width = samples.shape[1]
    capacity = CAP
    centers = old_centroids.shape[1]
    share_rows = centers // members
    position = jnp.arange(row_count, dtype=jnp.int32)
    is_live = position < live_rows[0]
    group_id = coarse_label[:, 0]
    member_of = (
        (group_id[:, None] == jnp.arange(groups, dtype=jnp.int32)[None, :]) & is_live[:, None]
    ).astype(jnp.int32)
    before = jnp.cumsum(member_of, axis=0) - member_of
    slot_index = jnp.sum(before * member_of, axis=1)
    target = jnp.where(is_live, group_id * capacity + slot_index, groups * capacity)
    outgoing = (
        jnp.zeros((groups * capacity, width), samples.dtype).at[target].set(samples, mode="drop")
    )
    out_labels = (
        jnp.full((groups * capacity,), -1, jnp.int32).at[target].set(fine_label, mode="drop")
    )
    arrived, arrived_labels = (
        lax.all_to_all(
            outgoing.reshape(groups, capacity, width),
            "coarse",
            split_axis=0,
            concat_axis=0,
            tiled=True,
        ),
        lax.all_to_all(
            out_labels.reshape(groups, capacity), "coarse", split_axis=0, concat_axis=0, tiled=True
        ),
    )
    arrived = arrived.reshape(groups * capacity, width)
    arrived_labels = arrived_labels.reshape(groups * capacity)
    selector = arrived_labels[None, :] == jnp.arange(centers, dtype=jnp.int32)[:, None]
    totals = jnp.dot(selector.astype(jnp.bfloat16), arrived, preferred_element_type=jnp.float32)
    counts = jnp.sum(selector.astype(jnp.float32), axis=1)
    start = member_index * share_rows
    summed, counted = (
        lax.psum(totals.astype(jnp.bfloat16), "member").astype(jnp.float32),
        lax.psum(counts.astype(jnp.bfloat16), "member").astype(jnp.float32),
    )
    renewed = (summed + prior_weight * old_centroids[0]) / (counted[:, None] + prior_weight)
    share = lax.dynamic_slice_in_dim(renewed, start, share_rows, 0)
    centroid_bf = renewed.astype(jnp.bfloat16)
    half_norm = 0.5 * jnp.sum(jnp.square(centroid_bf.astype(jnp.float32)), axis=1)
    scored = (
        lax.dot_general(
            arrived, centroid_bf, (((1,), (1,)), ((), ())), preferred_element_type=jnp.float32
        )
        - half_norm[None, :]
    )
    returned = lax.all_to_all(
        scored.astype(jnp.bfloat16).reshape(groups, capacity, centers),
        "coarse",
        split_axis=0,
        concat_axis=0,
        tiled=True,
    )
    flattened = returned.reshape(groups * capacity, centers)
    padded = jnp.concatenate([flattened, jnp.zeros((1, centers), jnp.bfloat16)], axis=0)
    scores = padded[target]
    return (scores, share[None])


def solution(mesh):
    return jax.shard_map(
        per_device,
        mesh=mesh,
        in_specs=(
            P(("coarse", "member"), None),
            P(("coarse", "member"), None),
            P(("coarse", "member")),
            P(("coarse", "member")),
            P("coarse", None, None),
        ),
        out_specs=(P(("coarse", "member"), None), P("coarse", "member", None)),
        check_vma=False,
    )
```

profile of v0, /device:TPU:0, one launch (start us, length us, event | category | flops | bytes accessed | tf_op | source)
XLA Modules:
  0.0 288.5 jit_solution(2461157060050382578)
XLA Ops:
  7.8 0.7 reduce
  8.6 1.2 reduce-window.6
  9.7 0.2 slice_reduce_fusion
  9.9 0.2 reduce-window.9
  10.1 0.1 add_bitcast_fusion
  10.2 0.7 fusion.14
  11.0 5.4 %scatter_custom_fusion.1 = s32[1920]{0:T(1024)S(1)} fusion(s32[1280]{0:T(1024)S(1)} %get-tuple-element.3, s32[1280]{0:T(1024)} %param.7, s32[]{:T(128)} %constant.17.clone.1), kind=kCustom, calls=%fused_computation.36 | custom fusion | bytes 8192 | tf_op jit(solution)/shard_map/scatter | solution.py:32
  16.4 0.7 all_to_all.13
  17.1 6.3 %all-to-all-start.1 = ((s32[4,1,480]{2,1,0:T(1,128)}), s32[4,1,480]{2,1,0:T(1,128)S(1)}, u32[]{:S(2)}, u32[]{:S(2)}) async-start(s32[4,1,480]{2,1,0:T(1,128)} %all_to_all.13), calls=%async_computation.1 | async-start | bytes 16384 | tf_op jit(solution)/shard_map/all_to_all | solution.py:42
  23.4 10.7 %scatter_custom_fusion = bf16[1920,768]{1,0:T(8,128)(2,1)} fusion(s32[1280]{0:T(1024)S(1)} %get-tuple-element.3, bf16[1280,768]{1,0:T(8,128)(2,1)} %param.5, bf16[]{:T(256)} %constant.12.clone.1), kind=kCustom, calls=%fused_computation.12 | custom fusion | bytes 2949632 | tf_op jit(solution)/shard_map/scatter | solution.py:29
  34.1 0.0 all-to-all-done.1
  34.1 5.1 %all-to-all-start = ((bf16[4,480,768]{2,1,0:T(8,128)(2,1)}), bf16[4,480,768]{2,1,0:T(8,128)(2,1)S(1)}, u32[]{:S(2)}, u32[]{:S(2)}) async-start(bf16[4,480,768]{2,1,0:T(8,128)(2,1)} %bitcast.2), calls=%async_computation | async-start | bytes 5898240 | tf_op jit(solution)/shard_map/all_to_all | solution.py:35
  39.2 0.0 all-reduce.3.cloned.1.call-start
  39.2 0.1 eq.48
  39.3 65.8 %all-to-all-done = bf16[4,480,768]{2,1,0:T(8,128)(2,1)S(1)} async-done(((bf16[4,480,768]{2,1,0:T(8,128)(2,1)}), bf16[4,480,768]{2,1,0:T(8,128)(2,1)S(1)}, u32[]{:S(2)}, u32[]{:S(2)}) %all-to-all-start) | async-done | bytes 2949152 | tf_op jit(solution)/shard_map/all_to_all | solution.py:35
  105.1 0.0 copy-start
  105.1 4.7 %fusion.3 = bf16[1024,768]{1,0:T(8,128)(2,1)} fusion(bf16[1920,768]{1,0:T(8,128)(2,1)S(1)} %bitcast.40, s32[1920]{0:T(1024)S(1)} %eq.48), kind=kOutput, calls=%fused_computation.11 | convolution fusion | flops 3022651392 | bytes 4529664 | tf_op jit(solution)/shard_map/dot_general | solution.py:49
  109.7 0.0 copy-done
  109.7 0.0 all-reduce.3.cloned.1.call-update
  109.8 0.9 convert_reduce_fusion
  110.6 13.2 %psum.15 = bf16[1024]{0:T(1024)(128)(2,1)S(1)} all-reduce(bf16[1024]{0:T(1024)(128)(2,1)S(1)} %convert_reduce_fusion), channel_id=1, replica_groups=mesh['coarse'=4,'member'=8] {'member'}, use_global_device_ids=true, to_apply=%region_7.8 | all-reduce | flops 1024 | bytes 4096 | tf_op jit(solution)/shard_map/psum | solution.py:54
  123.9 44.2 %all-reduce.3.cloned.1.call-done = bf16[1024,768]{1,0:T(8,128)(2,1)} async-done(((bf16[1024,768]{1,0:T(8,128)(2,1)}), bf16[1024,768]{1,0:T(8,128)(2,1)}) %all-reduce.3.cloned.1.call-update) | async-done | bytes 1572880 | tf_op jit(solution)/shard_map/psum | solution.py:53
  168.1 0.0 copy-start.1
  168.1 3.2 %multiply_reduce_fusion = (f32[1024]{0:T(1024)S(1)}, f32[1024,768]{1,0:T(8,128)S(1)}) fusion(f32[1024]{0:T(1024)S(1)} %convert_add_fusion, f32[1,1024,768]{2,1,0:T(8,128)} %param.9, bf16[1024,768]{1,0:T(8,128)(2,1)} %all-reduce.3.cloned.1.call-done), kind=kLoop, calls=%fused_computation.10 | loop fusion | flops 6290432 | bytes 7872512 | tf_op jit(solution)/shard_map/reduce_sum | solution.py:59
  171.3 0.0 copy-done.1
  171.3 4.9 %subtract_convert_fusion = bf16[1920,1024]{1,0:T(8,128)(2,1)} fusion(f32[1024]{0:T(1024)S(1)} %broadcast_multiply_fusion, bf16[1920,768]{1,0:T(8,128)(2,1)S(1)} %bitcast.41, f32[1024,768]{1,0:T(8,128)S(1)} %get-tuple-element.5), kind=kOutput, calls=%fused_computation.3 | convolution fusion | flops 3024617472 | bytes 10031104 | tf_op jit(solution)/shard_map/dot_general | solution.py:61
  176.2 4.8 %all-to-all-start.2 = ((bf16[4,480,1024]{2,1,0:T(8,128)(2,1)}), bf16[4,480,1024]{2,1,0:T(8,128)(2,1)}, u32[]{:S(2)}, u32[]{:S(2)}) async-start(bf16[4,480,1024]{2,1,0:T(8,128)(2,1)} %bitcast.39), calls=%async_computation.2 | async-start | bytes 7864320 | tf_op jit(solution)/shard_map/all_to_all | solution.py:66
  181.1 0.8 dynamic-slice_bitcast_fusion
  181.9 86.1 %all-to-all-done.2 = bf16[4,480,1024]{2,1,0:T(8,128)(2,1)} async-done(((bf16[4,480,1024]{2,1,0:T(8,128)(2,1)}), bf16[4,480,1024]{2,1,0:T(8,128)(2,1)}, u32[]{:S(2)}, u32[]{:S(2)}) %all-to-all-start.2) | async-done | bytes 3932192 | tf_op jit(solution)/shard_map/all_to_all | solution.py:66
  267.9 4.4 %concatenate.3 = bf16[1921,1024]{1,0:T(8,128)(2,1)} pad(bf16[1920,1024]{1,0:T(8,128)(2,1)} %bitcast.6, bf16[]{:T(256)} %constant.12.clone.1), padding=0_1x0_0 | pad | bytes 7866370 | tf_op jit(solution)/shard_map/concatenate | solution.py:74
  272.3 9.3 %gather_fusion = bf16[1280,1024]{1,0:T(8,128)(2,1)} fusion(bf16[1921,1024]{1,0:T(8,128)(2,1)} %concatenate.3, s32[2048]{0:T(1024)S(1)} %pad_clamp_fusion), kind=kCustom, calls=%fused_computation | custom fusion | bytes 5248000 | tf_op jit(solution)/shard_map/gather | solution.py:75
  (8 shorter events, 0.1 us)
Async XLA Ops:
  17.1 17.0 %all-to-all-start.1 = ((s32[4,1,480]{2,1,0:T(1,128)}), s32[4,1,480]{2,1,0:T(1,128)S(1)}, u32[]{:S(2)}, u32[]{:S(2)}) async-start(s32[4,1,480]{2,1,0:T(1,128)} %all_to_all.13), calls=%async_computation.1 | async-start | bytes 16384 | tf_op jit(solution)/shard_map/all_to_all | solution.py:42
  34.1 71.0 %all-to-all-start = ((bf16[4,480,768]{2,1,0:T(8,128)(2,1)}), bf16[4,480,768]{2,1,0:T(8,128)(2,1)S(1)}, u32[]{:S(2)}, u32[]{:S(2)}) async-start(bf16[4,480,768]{2,1,0:T(8,128)(2,1)} %bitcast.2), calls=%async_computation | async-start | bytes 5898240 | tf_op jit(solution)/shard_map/all_to_all | solution.py:35
  39.2 128.9 %all-reduce.3.cloned.1.call-start = ((), (), s32[]{:S(2)}) async-start(), calls=%async_computation.3 | async-start | bytes 3145728 | tf_op jit(solution)/shard_map/psum | solution.py:53
  105.1 4.7 %copy-start = (bf16[4,480,768]{2,1,0:T(8,128)(2,1)}, bf16[4,480,768]{2,1,0:T(8,128)(2,1)S(1)}, u32[]{:S(2)}) copy-start(bf16[4,480,768]{2,1,0:T(8,128)(2,1)S(1)} %all-to-all-done) | copy-start | bytes 8847364
  168.1 3.3 %copy-start.1 = (bf16[4,480,768]{2,1,0:T(8,128)(2,1)S(1)}, bf16[4,480,768]{2,1,0:T(8,128)(2,1)}, u32[]{:S(2)}) copy-start(bf16[4,480,768]{2,1,0:T(8,128)(2,1)} %copy-done) | copy-start | bytes 8847364
  176.2 91.7 %all-to-all-start.2 = ((bf16[4,480,1024]{2,1,0:T(8,128)(2,1)}), bf16[4,480,1024]{2,1,0:T(8,128)(2,1)}, u32[]{:S(2)}, u32[]{:S(2)}) async-start(bf16[4,480,1024]{2,1,0:T(8,128)(2,1)} %bitcast.39), calls=%async_computation.2 | async-start | bytes 7864320 | tf_op jit(solution)/shard_map/all_to_all | solution.py:66
Sparse Core Ops, SparseCore 0:
  109.9 58.1 all-reduce.2
where the time goes:
time: 289 us; the launch traced here: 288 us
  waiting for transfers between devices  196 us (68%)
  local copies, waits for them, and re-layouts  31.6 us (11%)
  starting transfers between devices  16.2 us (6%)
  between operations  14.7 us (5%)
  blocking collectives  13.2 us (5%)
  matrix products  9.59 us (3%)
  other arithmetic  7.05 us (2%)
    all_to_all x1, waiting for transfers between devices, per_device(): lax.all_to_all(scored.astype(jnp.bfloat16).reshape(groups, capacity, cent...  86.1 us
    all_to_all x1, waiting for transfers between devices, per_device(): lax.all_to_all(outgoing.reshape(groups, capacity, width), 'coarse', split...  65.8 us
    psum x1, waiting for transfers between devices, per_device(): lax.psum(totals.astype(jnp.bfloat16), 'member').astype(jnp.float32)  44.2 us
    psum x1, blocking collectives, per_device(): lax.psum(counts.astype(jnp.bfloat16), 'member').astype(jnp.float32)  13.2 us
    scatter x1, local copies, waits for them, and re-layouts, per_device(): jnp.zeros((groups * capacity, width), samples.dtype).at[target]  10.7 us
    gather x1, local copies, waits for them, and re-layouts, per_device(): scores = padded[target]  9.32 us
    all_to_all x1, starting transfers between devices, per_device(): lax.all_to_all(out_labels.reshape(groups, capacity), 'coarse', split_axis...  6.32 us
  transfers between devices with their start and end apart: 4, of which 3 were waited for; matrix products, arithmetic and copies ran while one was open for 4% of the time, Pallas kernels for 0%

commit v1 on v0

--- a/solution.py
+++ b/solution.py
@@ -63,13 +63,19 @@
         )
         - half_norm[None, :]
     )
-    returned = lax.all_to_all(
-        scored.astype(jnp.bfloat16).reshape(groups, capacity, centers),
-        "coarse",
-        split_axis=0,
-        concat_axis=0,
-        tiled=True,
-    )
+    array = scored.astype(jnp.bfloat16).reshape(groups, capacity, centers)
+    ways, here = (lax.axis_size("coarse"), lax.axis_index("coarse"))
+    width_2 = array.shape[0] // ways
+    lengths = list(array.shape)
+    lengths[0] = width_2
+    height = lengths[0]
+    lengths[0] = height * ways
+    returned = jnp.zeros(lengths, array.dtype)
+    for mask in range(ways):
+        part = lax.dynamic_slice_in_dim(array, (here ^ mask) * width_2, width_2, axis=0)
+        if mask:
+            part = lax.ppermute(part, "coarse", [(d, d ^ mask) for d in range(ways)])
+        returned = lax.dynamic_update_slice_in_dim(returned, part, (here ^ mask) * height, axis=0)
     flattened = returned.reshape(groups * capacity, centers)
     padded = jnp.concatenate([flattened, jnp.zeros((1, centers), jnp.bfloat16)], axis=0)
     scores = padded[target]

time: 289 us -> 288 us (level)
  the two profiles are of different devices: /device:TPU:0 before, /device:TPU:8 now
where the time goes in v1:
time: 288 us
  waiting for transfers between devices  189 us (66%)
  local copies, waits for them, and re-layouts  42.7 us (15%)
  between operations  14.8 us (5%)
  starting transfers between devices  13.9 us (5%)
  blocking collectives  12.2 us (4%)
  matrix products  8.21 us (3%)
  other arithmetic  7.05 us (2%)
    ppermute x3, waiting for transfers between devices, per_device(): part = lax.ppermute(part, 'coarse', [(d, d ^ mask) for d in range(ways)])  78.4 us
    all_to_all x1, waiting for transfers between devices, per_device(): lax.all_to_all(outgoing.reshape(groups, capacity, width), 'coarse', split...  62.5 us
    psum x1, waiting for transfers between devices, per_device(): lax.psum(totals.astype(jnp.bfloat16), 'member').astype(jnp.float32)  48 us
    psum x1, blocking collectives, per_device(): lax.psum(counts.astype(jnp.bfloat16), 'member').astype(jnp.float32)  12.2 us
    scatter x1, local copies, waits for them, and re-layouts, per_device(): jnp.zeros((groups * capacity, width), samples.dtype).at[target]  10.7 us
    gather x1, local copies, waits for them, and re-layouts, per_device(): scores = padded[target]  9.32 us
    dynamic_update_slice x3, local copies, waits for them, and re-layouts, per_device(): lax.dynamic_update_slice_in_dim(returned, part, (here ^ mask) * height, a...  6.66 us
  transfers between devices with their start and end apart: 6, of which 5 were waited for; matrix products, arithmetic and copies ran while one was open for 6% of the time, Pallas kernels for 0%

profile of v1, /device:TPU:8, one launch (start us, length us, event | category | flops | bytes accessed | tf_op | source)
XLA Modules:
  0.0 287.8 jit_solution(15073573142965333502)
XLA Ops:
  7.8 0.7 reduce
  8.6 1.2 reduce-window.6
  9.7 0.2 slice_reduce_fusion
  9.9 0.2 reduce-window.9
  10.1 0.1 add_bitcast_fusion
  10.2 0.7 fusion.14
  11.0 5.4 %scatter_custom_fusion.1 = s32[1920]{0:T(1024)S(1)} fusion(s32[1280]{0:T(1024)S(1)} %get-tuple-element.3, s32[1280]{0:T(1024)} %param.7, s32[]{:T(128)} %constant.22.clone.1), kind=kCustom, calls=%fused_computation.37 | custom fusion | bytes 8192 | tf_op jit(solution)/shard_map/scatter | solution.py:32
  16.4 0.7 all_to_all.10
  17.1 5.3 %all-to-all-start.1 = ((s32[4,1,480]{2,1,0:T(1,128)}), s32[4,1,480]{2,1,0:T(1,128)S(1)}, u32[]{:S(2)}, u32[]{:S(2)}) async-start(s32[4,1,480]{2,1,0:T(1,128)} %all_to_all.10), calls=%async_computation.1 | async-start | bytes 16384 | tf_op jit(solution)/shard_map/all_to_all | solution.py:42
  22.4 10.7 %scatter_custom_fusion = bf16[1920,768]{1,0:T(8,128)(2,1)} fusion(s32[1280]{0:T(1024)S(1)} %get-tuple-element.3, bf16[1280,768]{1,0:T(8,128)(2,1)} %param.5, bf16[]{:T(256)} %constant.17.clone.1), kind=kCustom, calls=%fused_computation.12 | custom fusion | bytes 2949632 | tf_op jit(solution)/shard_map/scatter | solution.py:29
  33.1 0.0 all-to-all-done.1
  33.1 5.1 %all-to-all-start = ((bf16[4,480,768]{2,1,0:T(8,128)(2,1)}), bf16[4,480,768]{2,1,0:T(8,128)(2,1)S(1)}, u32[]{:S(2)}, u32[]{:S(2)}) async-start(bf16[4,480,768]{2,1,0:T(8,128)(2,1)} %bitcast.2), calls=%async_computation | async-start | bytes 5898240 | tf_op jit(solution)/shard_map/all_to_all | solution.py:35
  38.2 0.0 all-reduce.3.cloned.1.call-start
  38.2 0.1 eq.48
  38.3 62.5 %all-to-all-done = bf16[4,480,768]{2,1,0:T(8,128)(2,1)S(1)} async-done(((bf16[4,480,768]{2,1,0:T(8,128)(2,1)}), bf16[4,480,768]{2,1,0:T(8,128)(2,1)S(1)}, u32[]{:S(2)}, u32[]{:S(2)}) %all-to-all-start) | async-done | bytes 2949152 | tf_op jit(solution)/shard_map/all_to_all | solution.py:35
  100.8 0.0 copy-start
  100.8 4.7 %fusion.3 = bf16[1024,768]{1,0:T(8,128)(2,1)} fusion(bf16[1920,768]{1,0:T(8,128)(2,1)S(1)} %bitcast.40, s32[1920]{0:T(1024)S(1)} %eq.48), kind=kOutput, calls=%fused_computation.11 | convolution fusion | flops 3022651392 | bytes 4529664 | tf_op jit(solution)/shard_map/dot_general | solution.py:49
  105.5 0.0 copy-done
  105.5 0.0 all-reduce.3.cloned.1.call-update
  105.5 0.9 convert_reduce_fusion
  106.4 12.2 %psum.15 = bf16[1024]{0:T(1024)(128)(2,1)S(1)} all-reduce(bf16[1024]{0:T(1024)(128)(2,1)S(1)} %convert_reduce_fusion), channel_id=1, replica_groups=mesh['coarse'=4,'member'=8] {'member'}, use_global_device_ids=true, to_apply=%region_7.8 | all-reduce | flops 1024 | bytes 4096 | tf_op jit(solution)/shard_map/psum | solution.py:54
  118.6 48.0 %all-reduce.3.cloned.1.call-done = bf16[1024,768]{1,0:T(8,128)(2,1)} async-done(((bf16[1024,768]{1,0:T(8,128)(2,1)}), bf16[1024,768]{1,0:T(8,128)(2,1)}) %all-reduce.3.cloned.1.call-update) | async-done | bytes 1572880 | tf_op jit(solution)/shard_map/psum | solution.py:53
  166.7 0.0 copy-start.1
  166.7 3.2 %multiply_reduce_fusion = (f32[1024]{0:T(1024)S(1)}, f32[1024,768]{1,0:T(8,128)S(1)}) fusion(f32[1024]{0:T(1024)S(1)} %convert_add_fusion, f32[1,1024,768]{2,1,0:T(8,128)} %param.9, bf16[1024,768]{1,0:T(8,128)(2,1)} %all-reduce.3.cloned.1.call-done), kind=kLoop, calls=%fused_computation.10 | loop fusion | flops 6290432 | bytes 7872512 | tf_op jit(solution)/shard_map/reduce_sum | solution.py:59
  169.9 0.0 copy-done.1
  169.9 3.5 %subtract_convert_fusion = bf16[1920,1024]{1,0:T(8,128)(2,1)S(1)} fusion(f32[1024]{0:T(1024)S(1)} %broadcast_multiply_fusion, bf16[1920,768]{1,0:T(8,128)(2,1)S(1)} %bitcast.41, f32[1024,768]{1,0:T(8,128)S(1)} %get-tuple-element.5), kind=kOutput, calls=%fused_computation.3 | convolution fusion | flops 3024617472 | bytes 10031104 | tf_op jit(solution)/shard_map/dot_general | solution.py:61
  173.5 2.4 broadcast_in_dim.12
  175.8 2.0 constant_dynamic-slice_fusion
  177.9 0.4 collective-permute-start
  178.2 2.6 collective-permute-start.1
  180.8 0.6 collective-permute-start.2
  181.3 0.8 dynamic-slice_bitcast_fusion
  182.1 36.1 %collective-permute-done = bf16[1,480,1024]{2,1,0:T(8,128)(2,1)} collective-permute-done((bf16[1,480,1024]{2,1,0:T(8,128)(2,1)}, bf16[1,480,1024]{2,1,0:T(8,128)(2,1)}, u32[]{:S(2)}, u32[]{:S(2)}) %collective-permute-start) | collective-permute-done | bytes 983072 | tf_op jit(solution)/shard_map/ppermute | solution.py:77
  218.2 2.2 constant_dynamic-update-slice_fusion.2
  220.4 25.0 %collective-permute-done.1 = bf16[1,480,1024]{2,1,0:T(8,128)(2,1)} collective-permute-done((bf16[1,480,1024]{2,1,0:T(8,128)(2,1)}, bf16[1,480,1024]{2,1,0:T(8,128)(2,1)}, u32[]{:S(2)}, u32[]{:S(2)}) %collective-permute-start.1) | collective-permute-done | bytes 983072 | tf_op jit(solution)/shard_map/ppermute | solution.py:77
  245.4 2.2 constant_dynamic-update-slice_fusion.1
  247.7 17.3 %collective-permute-done.2 = bf16[1,480,1024]{2,1,0:T(8,128)(2,1)} collective-permute-done((bf16[1,480,1024]{2,1,0:T(8,128)(2,1)}, bf16[1,480,1024]{2,1,0:T(8,128)(2,1)}, u32[]{:S(2)}, u32[]{:S(2)}) %collective-permute-start.2) | collective-permute-done | bytes 983072 | tf_op jit(solution)/shard_map/ppermute | solution.py:77
  264.9 2.2 constant_dynamic-update-slice_fusion
  267.2 4.4 %concatenate.3 = bf16[1921,1024]{1,0:T(8,128)(2,1)} pad(bf16[1920,1024]{1,0:T(8,128)(2,1)} %bitcast.6, bf16[]{:T(256)} %constant.17.clone.1), padding=0_1x0_0 | pad | bytes 7866370 | tf_op jit(solution)/shard_map/concatenate | solution.py:80
  271.6 9.3 %gather_fusion = bf16[1280,1024]{1,0:T(8,128)(2,1)} fusion(bf16[1921,1024]{1,0:T(8,128)(2,1)} %concatenate.3, s32[2048]{0:T(1024)S(1)} %pad_clamp_fusion), kind=kCustom, calls=%fused_computation | custom fusion | bytes 5248000 | tf_op jit(solution)/shard_map/gather | solution.py:81
  (8 shorter events, 0.1 us)
Async XLA Ops:
  17.1 16.0 %all-to-all-start.1 = ((s32[4,1,480]{2,1,0:T(1,128)}), s32[4,1,480]{2,1,0:T(1,128)S(1)}, u32[]{:S(2)}, u32[]{:S(2)}) async-start(s32[4,1,480]{2,1,0:T(1,128)} %all_to_all.10), calls=%async_computation.1 | async-start | bytes 16384 | tf_op jit(solution)/shard_map/all_to_all | solution.py:42
  33.1 67.7 %all-to-all-start = ((bf16[4,480,768]{2,1,0:T(8,128)(2,1)}), bf16[4,480,768]{2,1,0:T(8,128)(2,1)S(1)}, u32[]{:S(2)}, u32[]{:S(2)}) async-start(bf16[4,480,768]{2,1,0:T(8,128)(2,1)} %bitcast.2), calls=%async_computation | async-start | bytes 5898240 | tf_op jit(solution)/shard_map/all_to_all | solution.py:35
  38.2 128.5 %all-reduce.3.cloned.1.call-start = ((), (), s32[]{:S(2)}) async-start(), calls=%async_computation.2 | async-start | bytes 3145728 | tf_op jit(solution)/shard_map/psum | solution.py:53
  100.8 4.7 %copy-start = (bf16[4,480,768]{2,1,0:T(8,128)(2,1)}, bf16[4,480,768]{2,1,0:T(8,128)(2,1)S(1)}, u32[]{:S(2)}) copy-start(bf16[4,480,768]{2,1,0:T(8,128)(2,1)S(1)} %all-to-all-done) | copy-start | bytes 8847364
  166.7 3.3 %copy-start.1 = (bf16[4,480,768]{2,1,0:T(8,128)(2,1)S(1)}, bf16[4,480,768]{2,1,0:T(8,128)(2,1)}, u32[]{:S(2)}) copy-start(bf16[4,480,768]{2,1,0:T(8,128)(2,1)} %copy-done) | copy-start | bytes 8847364
  177.9 40.4 %collective-permute-start = (bf16[1,480,1024]{2,1,0:T(8,128)(2,1)}, bf16[1,480,1024]{2,1,0:T(8,128)(2,1)}, u32[]{:S(2)}, u32[]{:S(2)}) collective-permute-start(bf16[1,480,1024]{2,1,0:T(8,128)(2,1)} %get-tuple-element.8), channel_id=1, source_target_pairs={{0,8},{8,0},{16,24},{24,16},{1,9},{9,1},{17,25},{25,17},{2,10},{10... | collective-permute-start | bytes 2949128 | tf_op jit(solution)/shard_map/ppermute | solution.py:77
  178.2 67.2 %collective-permute-start.1 = (bf16[1,480,1024]{2,1,0:T(8,128)(2,1)}, bf16[1,480,1024]{2,1,0:T(8,128)(2,1)}, u32[]{:S(2)}, u32[]{:S(2)}) collective-permute-start(bf16[1,480,1024]{2,1,0:T(8,128)(2,1)} %get-tuple-element.7), channel_id=1, source_target_pairs={{0,16},{8,24},{16,0},{24,8},{1,17},{9,25},{17,1},{25,9},{2,18},{10... | collective-permute-start | bytes 2949128 | tf_op jit(solution)/shard_map/ppermute | solution.py:77
  180.8 84.2 %collective-permute-start.2 = (bf16[1,480,1024]{2,1,0:T(8,128)(2,1)}, bf16[1,480,1024]{2,1,0:T(8,128)(2,1)}, u32[]{:S(2)}, u32[]{:S(2)}) collective-permute-start(bf16[1,480,1024]{2,1,0:T(8,128)(2,1)} %get-tuple-element.6), channel_id=1, source_target_pairs={{0,24},{8,16},{16,8},{24,0},{1,25},{9,17},{17,9},{25,1},{2,26},{10... | collective-permute-start | bytes 2949128 | tf_op jit(solution)/shard_map/ppermute | solution.py:77
Sparse Core Ops, SparseCore 0:
  105.6 61.0 all-reduce.2
